TPU v7x, 256 devices: a whole 4x4x8 slice. The times are simulated.
256 devices in a mesh: basis: 32 (over x, z), tile: 8 (over y, core).
Axes of the slice: x: 4, y: 4, z: 8, core: 2. Of those that a mesh axis runs over, the one named last changes fastest.
Arguments:
- lower_vectors: bfloat16 [1536, 256, 256], P('basis'), may hold values from -0.005859375 to 0.005859375
- upper_vectors: bfloat16 [1024, 256, 1024], P('basis', None, 'tile'), may hold values from -6 to 6
- dipole_vib: bfloat16 [3, 256, 256], replicated, may hold values from -0.375 to 0.375
- rot_factor: float32 [1536, 3], P('basis'), may hold values from 0.5 to 1.5
- coupling: int32 [1536, 3], P('basis'), may hold values 0 or 1
- lower_sizes: int32 [1536], P('basis'), may hold values from 128 to 256
- upper_sizes: int32 [1024], P('basis'), may hold values from 128 to 256
- lower_range: int32 [32, 2], P('basis'), may hold values from 0 to 1024, as said below
Outputs:
- strength: float32 [256, 1024], P('basis', 'tile')
- average: float32 [256], P('basis')
Inputs may be any that keep to these rules, and one draw needn't show every extreme that they name: `lower_range`: the ranges are contiguous in device order and cover 0 to 1024; device j starts within 8 blocks of j * 32 (device 0 at 0); at least one device holds exactly 48 blocks, and none holds more.
All inputs are finite; a program needn't handle non-finite values. No bound on the sum of `coupling` on one device may be relied on, other than what follows from the above.
Results may differ from a plain program's by a relative error of at most 0.0065.
Values may be sent and summed in bfloat16 or wider, within the bound.
No kernel may reach another device: no remote copies, remote signals or barrier semaphores. Data moves between devices by JAX's collectives and lax.ppermute only.
A program may use at most 128 MiB of HBM per device.

v0:
```python
import jax
import jax.numpy as jnp
from jax import lax
from jax.experimental import pallas as pl
from jax.experimental.pallas import tpu as pltpu
from jax.sharding import PartitionSpec as P

NUP = 1024
SHIFT = 8
MARGIN = SHIFT + 1
CHUNK = 12
AHEAD = 2
LEAST = 128
VMEM_BYTES = 28 * 1024 * 1024
BF16 = jnp.bfloat16
F32 = jnp.float32


def vmem_spec():
    return pl.BlockSpec(memory_space=pltpu.VMEM)


def smem_spec():
    return pl.BlockSpec(memory_space=pltpu.SMEM)


def any_spec():
    return pl.BlockSpec(memory_space=pl.ANY)


def in_hbm(array):
    return pltpu.with_memory_space_constraint(array, pltpu.HBM)


def in_vmem(array):
    return pltpu.with_memory_space_constraint(array, pltpu.VMEM)


def edges_kernel(sizes_hbm, upper, low, high, sizes, sems):
    blocks, rows, columns = upper.shape
    margin = low.shape[0]
    copies = [
        pltpu.make_async_copy(upper.at[pl.ds(blocks - margin, margin)], low, sems.at[0]),
        pltpu.make_async_copy(upper.at[pl.ds(0, margin)], high, sems.at[1]),
    ]
    known = pltpu.make_async_copy(sizes_hbm, sizes, sems.at[2])
    known.start()
    for copy in copies:
        copy.start()
    row_ids = LEAST + lax.broadcasted_iota(jnp.int32, (rows - LEAST, columns), 0)
    known.wait()
    for copy, out, first in zip(copies, (low, high), (blocks - margin, 0)):
        copy.wait()
        for block in range(margin):
            out[block, LEAST:] = jnp.where(
                row_ids < sizes[first + block], out[block, LEAST:], jnp.zeros((), BF16)
            )


def edges(upper_sizes, upper_vectors):
    blocks, rows, columns = upper_vectors.shape
    shape = pltpu.VMEM((MARGIN, rows, columns), BF16)
    return pl.pallas_call(
        edges_kernel,
        out_shape=(shape, shape),
        in_specs=[any_spec(), any_spec()],
        out_specs=(vmem_spec(), vmem_spec()),
        scratch_shapes=[
            pltpu.SMEM((blocks,), jnp.int32),
            pltpu.SemaphoreType.DMA((3,)),
        ],
        name="edges",
    )(in_hbm(upper_sizes), in_hbm(upper_vectors))


def masked(block, size):
    rows, columns = block.shape
    row_ids = LEAST + lax.broadcasted_iota(jnp.int32, (rows - LEAST, columns), 0)
    tail = jnp.where(row_ids < size, block[LEAST:], jnp.zeros((), BF16))
    return jnp.concatenate([block[:LEAST], tail], axis=0)


def inner_kernel(
    first_ref,
    range_ref,
    rot,
    coupling,
    lower_sizes,
    upper_sizes,
    lower_hbm,
    upper_hbm,
    dipole_hbm,
    outer,
    partial,
    images,
    turned,
    lower,
    upper,
    dipole,
    sems,
):
    slots, rows, states = lower.shape
    blocks, _, columns = upper.shape
    start = range_ref[0, 0]
    count = range_ref[0, 1] - start
    base = start - first_ref[0] + MARGIN
    chunks = slots // CHUNK
    copies = [
        pltpu.make_async_copy(
            lower_hbm.at[pl.ds(chunk * CHUNK, CHUNK)],
            lower.at[pl.ds(chunk * CHUNK, CHUNK)],
            sems.at[chunk],
        )
        for chunk in range(chunks)
    ]
    copies.append(pltpu.make_async_copy(upper_hbm, upper, sems.at[chunks]))
    first_copy = pltpu.make_async_copy(dipole_hbm, dipole, sems.at[chunks + 1])
    first_copy.start()
    for copy in copies[:AHEAD]:
        copy.start()
    for index in range(2 * MARGIN):
        images[index] = jnp.zeros((rows, states), BF16)
    first_copy.wait()
    for d in range(3):
        turned[d] = dipole[d].T
    nearer = jnp.zeros((rows, states), F32)
    further = jnp.zeros((rows, states), F32)
    for slot in range(slots):
        if slot % CHUNK == 0:
            chunk = slot // CHUNK
            copies[chunk].wait()
            if chunk + AHEAD < len(copies):
                copies[chunk + AHEAD].start()
        live = masked(lower[slot], lower_sizes[slot])
        parts = []
        for d in range(3):
            factor = rot[d, slot] * coupling[d, slot].astype(F32)
            factor = jnp.where(slot < count, factor, 0.0)
            parts.append(factor * jnp.dot(turned[d], live, preferred_element_type=F32))
        images[base + (slot - 1)] = (nearer + parts[0]).astype(BF16)
        nearer = further + parts[1]
        further = parts[2]
    images[base + (slots - 1)] = nearer.astype(BF16)
    images[base + slots] = further.astype(BF16)
    for chunk in range(chunks, len(copies)):
        copies[chunk].wait()
    total = jnp.zeros((columns, states), F32)
    for block in range(blocks):
        live = masked(upper[block], upper_sizes[block])
        total += jnp.dot(live.T, images[MARGIN + block], preferred_element_type=F32)
    partial[...] = total.T
    for index in range(MARGIN):
        outer[index] = images[index].T
        outer[MARGIN + index] = images[MARGIN + blocks + index].T


def inner(first, lower_range, rot, coupling, lower_sizes, upper_sizes, lower, upper, dipole):
    slots, rows, states = lower.shape
    blocks, _, columns = upper.shape
    small = [in_hbm(a) for a in (lower_range, rot, coupling, lower_sizes, upper_sizes)]
    return pl.pallas_call(
        inner_kernel,
        out_shape=(
            pltpu.VMEM((2 * MARGIN, states, rows), BF16),
            pltpu.VMEM((states, columns), F32),
        ),
        in_specs=[smem_spec() for _ in range(6)] + [any_spec() for _ in range(3)],
        out_specs=(vmem_spec(), vmem_spec()),
        scratch_shapes=[
            pltpu.VMEM((slots + 2 * MARGIN + 2, rows, states), BF16),
            pltpu.VMEM((3, rows, rows), BF16),
            pltpu.VMEM(lower.shape, BF16),
            pltpu.VMEM(upper.shape, BF16),
            pltpu.VMEM(dipole.shape, BF16),
            pltpu.SemaphoreType.DMA((slots // CHUNK + 2,)),
        ],
        compiler_params=pltpu.CompilerParams(vmem_limit_bytes=VMEM_BYTES),
        name="inner",
    )(first, *small, in_hbm(lower), in_hbm(upper), in_hbm(dipole))


def outer_kernel(low, high, images, partial, out):
    total = partial[...]
    margin = low.shape[0]
    for index in range(margin):
        total += jnp.dot(images[index], low[index], preferred_element_type=F32)
    for index in range(margin):
        total += jnp.dot(images[margin + index], high[index], preferred_element_type=F32)
    out[...] = total.reshape(out.shape).astype(out.dtype)


def outer(low, high, images, partial, parts):
    states, columns = partial.shape
    return pl.pallas_call(
        outer_kernel,
        out_shape=pltpu.VMEM((parts, states // parts, columns), BF16),
        in_specs=[vmem_spec() for _ in range(4)],
        out_specs=vmem_spec(),
        compiler_params=pltpu.CompilerParams(vmem_limit_bytes=VMEM_BYTES),
        name="outer",
    )(in_vmem(low), in_vmem(high), images, partial)


def square_kernel(received, strength, sums):
    moment = jnp.sum(received[...].astype(F32), axis=0)
    squared = moment * moment
    strength[...] = squared
    row = jnp.sum(squared.T, axis=0, keepdims=True) * (1.0 / NUP)
    sums[...] = jnp.broadcast_to(row[None], sums.shape)


def square(received, tiles):
    _, band, columns = received.shape
    return pl.pallas_call(
        square_kernel,
        out_shape=(
            pltpu.VMEM((band, columns), F32),
            pltpu.VMEM((tiles, 1, band), F32),
        ),
        in_specs=[vmem_spec()],
        out_specs=(vmem_spec(), vmem_spec()),
        name="square",
    )(in_vmem(received))


def shards(
    lower_vectors,
    upper_vectors,
    dipole_vib,
    rot_factor,
    coupling,
    lower_sizes,
    upper_sizes,
    lower_range,
):
    parts = lax.axis_size("basis")
    tiles = lax.axis_size("tile")
    blocks = upper_vectors.shape[0]
    first = (lax.axis_index("basis") * blocks).astype(jnp.int32).reshape(1)
    forward = [(i, i + 1) for i in range(parts - 1)]
    backward = [(target, source) for source, target in forward]
    last_blocks, first_blocks = edges(upper_sizes, upper_vectors)
    low = lax.ppermute(last_blocks, "basis", forward)
    high = lax.ppermute(first_blocks, "basis", backward)
    images, partial = inner(
        first,
        lower_range,
        rot_factor.T,
        coupling.T,
        lower_sizes,
        upper_sizes,
        lower_vectors,
        upper_vectors,
        dipole_vib,
    )
    mine = outer(low, high, images, partial, parts)
    received = lax.all_to_all(mine, "basis", 0, 0, tiled=True)
    strength, sums = square(received, tiles)
    gathered = lax.all_to_all(sums, "tile", 0, 0, tiled=True)
    average = jnp.sum(gathered[:, 0, :], axis=0)
    return (strength, average)


def solution(mesh):
    in_specs = (
        P("basis", None, None),
        P("basis", None, "tile"),
        P(),
        P("basis", None),
        P("basis", None),
        P("basis"),
        P("basis"),
        P("basis", None),
    )
    out_specs = (P("basis", "tile"), P("basis"))
    return jax.shard_map(shards, mesh=mesh, in_specs=in_specs, out_specs=out_specs, check_vma=False)
```

profile of v0, /device:TPU:1, one launch (start us, length us, event | category | flops | bytes accessed | tf_op | source)
XLA Modules:
  0.0 56.1 jit_solution(12196543190780799420)
XLA Ops:
  0.6 1.4 %edges.1 = (bf16[9,256,128]{2,1,0:T(8,128)(2,1)S(1)}, bf16[9,256,128]{2,1,0:T(8,128)(2,1)S(1)}) custom-call(s32[32]{0:T(128)} %upper_sizes.1, bf16[32,256,128]{2,1,0:T(8,128)(2,1)} %upper_hbm.1), custom_call_target="tpu_custom_call" | custom-call | tf_op jit(solution)/shard_map/edges/pallas_call | solution.py:63
  2.0 4.4 %collective-permute-start = (bf16[9,256,128]{2,1,0:T(8,128)(2,1)S(1)}, bf16[9,256,128]{2,1,0:T(8,128)(2,1)S(1)}, u32[]{:S(2)}, u32[]{:S(2)}) collective-permute-start(bf16[9,256,128]{2,1,0:T(8,128)(2,1)S(1)} %get-tuple-element.8), channel_id=1, source_target_pairs={{0,8},{8,16},{16,24},{24,32},{32,40},{40,48},{48,56},{56,64},{64,7... | collective-permute-start | bytes 1769480 | tf_op jit(solution)/shard_map/ppermute | solution.py:243
  6.4 1.3 %collective-permute-start.1 = (bf16[9,256,128]{2,1,0:T(8,128)(2,1)S(1)}, bf16[9,256,128]{2,1,0:T(8,128)(2,1)S(1)}, u32[]{:S(2)}, u32[]{:S(2)}) collective-permute-start(bf16[9,256,128]{2,1,0:T(8,128)(2,1)S(1)} %get-tuple-element.9), channel_id=1, source_target_pairs={{8,0},{16,8},{24,16},{32,24},{40,32},{48,40},{56,48},{64,56},{72,6... | collective-permute-start | bytes 1769480 | tf_op jit(solution)/shard_map/ppermute | solution.py:244
  7.7 9.9 %inner.1 = (bf16[18,256,256]{2,1,0:T(8,128)(2,1)S(1)}, f32[256,128]{1,0:T(8,128)S(1)}) custom-call(s32[1]{0:T(128)} %bitcast.first_ref, s32[1,2]{1,0:T(1,128)} %range_ref.1, f32[3,48]{1,0:T(4,128)} %bitcast.3, s32[3,48]{1,0:T(4,128)} %bitcast.4, s32[48]{0:T(128)} %lower_sizes.1, s32[32]{0:T(128)} %upper_sizes.1, bf16[48,256,256]{2,1,0:T(8,128)(2,1)} %lower_hbm.1, ...), custom_call_target="tpu_custom_call" | custom-call | tf_op jit(solution)/shard_map/inner/pallas_call | solution.py:161
  17.6 0.8 %collective-permute-done.low = bf16[9,256,128]{2,1,0:T(8,128)(2,1)S(1)} collective-permute-done((bf16[9,256,128]{2,1,0:T(8,128)(2,1)S(1)}, bf16[9,256,128]{2,1,0:T(8,128)(2,1)S(1)}, u32[]{:S(2)}, u32[]{:S(2)}) %collective-permute-start) | collective-permute-done | bytes 589856 | tf_op jit(solution)/shard_map/ppermute | solution.py:243
  18.3 4.2 %collective-permute-done.1.high = bf16[9,256,128]{2,1,0:T(8,128)(2,1)S(1)} collective-permute-done((bf16[9,256,128]{2,1,0:T(8,128)(2,1)S(1)}, bf16[9,256,128]{2,1,0:T(8,128)(2,1)S(1)}, u32[]{:S(2)}, u32[]{:S(2)}) %collective-permute-start.1) | collective-permute-done | bytes 589856 | tf_op jit(solution)/shard_map/ppermute | solution.py:244
  22.5 0.8 %outer.1 = bf16[32,8,128]{2,1,0:T(8,128)(2,1)S(1)} custom-call(bf16[9,256,128]{2,1,0:T(8,128)(2,1)S(1)} %collective-permute-done.low, bf16[9,256,128]{2,1,0:T(8,128)(2,1)S(1)} %collective-permute-done.1.high, bf16[18,256,256]{2,1,0:T(8,128)(2,1)S(1)} %get-tuple-element.10.images, f32[256,128]{1,0:T(8,128)S(1)} %get-tuple-element.11.partial), custom_call_target="tpu_custom_call" | custom-call | tf_op jit(solution)/shard_map/outer/pallas_call | solution.py:194
  23.3 19.2 %all_to_all.10.received = bf16[32,8,128]{2,1,0:T(8,128)(2,1)S(1)} all-to-all(bf16[32,8,128]{2,1,0:T(8,128)(2,1)S(1)} %outer.1), channel_id=1, replica_groups=mesh['basis'=32,'tile'=8] {'basis'}, dimensions={0} | all-to-all | bytes 131072 | tf_op jit(solution)/shard_map/all_to_all | solution.py:257
  42.5 0.7 %square.1 = (f32[8,128]{1,0:T(8,128)S(1)}, f32[8,1,8]{2,1,0:T(1,128)}) custom-call(bf16[32,8,128]{2,1,0:T(8,128)(2,1)S(1)} %all_to_all.10.received), custom_call_target="tpu_custom_call" | custom-call | tf_op jit(solution)/shard_map/square/pallas_call | solution.py:214
  43.2 7.8 %all-to-all-start.1 = ((f32[8,1,8]{2,1,0:T(1,128)}), f32[8,1,8]{2,1,0:T(1,128)S(1)}, u32[]{:S(2)}, u32[]{:S(2)}) async-start(f32[8,1,8]{2,1,0:T(1,128)} %get-tuple-element.13), calls=%async_computation.1 | async-start | bytes 8192 | tf_op jit(solution)/shard_map/all_to_all | solution.py:259
  51.0 0.6 %copy.10 = f32[8,128]{1,0:T(8,128)} copy(f32[8,128]{1,0:T(8,128)S(1)} %get-tuple-element.14) | data formatting | bytes 8192
  51.6 4.0 %all-to-all-done.1 = f32[8,1,8]{2,1,0:T(1,128)S(1)} async-done(((f32[8,1,8]{2,1,0:T(1,128)}), f32[8,1,8]{2,1,0:T(1,128)S(1)}, u32[]{:S(2)}, u32[]{:S(2)}) %all-to-all-start.1) | async-done | bytes 288 | tf_op jit(solution)/shard_map/all_to_all | solution.py:259
  55.5 0.5 reduce_sum.9
Async XLA Ops:
  2.0 16.4 %collective-permute-start = (bf16[9,256,128]{2,1,0:T(8,128)(2,1)S(1)}, bf16[9,256,128]{2,1,0:T(8,128)(2,1)S(1)}, u32[]{:S(2)}, u32[]{:S(2)}) collective-permute-start(bf16[9,256,128]{2,1,0:T(8,128)(2,1)S(1)} %get-tuple-element.8), channel_id=1, source_target_pairs={{0,8},{8,16},{16,24},{24,32},{32,40},{40,48},{48,56},{56,64},{64,7... | collective-permute-start | bytes 1769480 | tf_op jit(solution)/shard_map/ppermute | solution.py:243
  6.4 16.1 %collective-permute-start.1 = (bf16[9,256,128]{2,1,0:T(8,128)(2,1)S(1)}, bf16[9,256,128]{2,1,0:T(8,128)(2,1)S(1)}, u32[]{:S(2)}, u32[]{:S(2)}) collective-permute-start(bf16[9,256,128]{2,1,0:T(8,128)(2,1)S(1)} %get-tuple-element.9), channel_id=1, source_target_pairs={{8,0},{16,8},{24,16},{32,24},{40,32},{48,40},{56,48},{64,56},{72,6... | collective-permute-start | bytes 1769480 | tf_op jit(solution)/shard_map/ppermute | solution.py:244
  43.2 12.3 %all-to-all-start.1 = ((f32[8,1,8]{2,1,0:T(1,128)}), f32[8,1,8]{2,1,0:T(1,128)S(1)}, u32[]{:S(2)}, u32[]{:S(2)}) async-start(f32[8,1,8]{2,1,0:T(1,128)} %get-tuple-element.13), calls=%async_computation.1 | async-start | bytes 8192 | tf_op jit(solution)/shard_map/all_to_all | solution.py:259
where the time goes:
time: 56.3 us; the launch traced here: 56.1 us
  blocking collectives  19.2 us (34%)
  starting transfers between devices  13.5 us (24%)
  Pallas kernels  12.7 us (23%)
  waiting for transfers between devices  8.9 us (16%)
  between operations  0.67 us (1%)
  local copies, waits for them, and re-layouts  0.59 us (1%)
    all_to_all x1, blocking collectives, shards(): received = lax.all_to_all(mine, 'basis', 0, 0, tiled=True)  19.2 us
    pallas_call x1, Pallas kernels, inner(): pl.pallas_call(inner_kernel, out_shape=(pltpu.VMEM((2 * MARGIN, states, r...  9.86 us
    all_to_all x1, starting transfers between devices, shards(): gathered = lax.all_to_all(sums, 'tile', 0, 0, tiled=True)  7.76 us
    ppermute x1, starting transfers between devices, shards(): low = lax.ppermute(last_blocks, 'basis', forward)  4.41 us
    ppermute x1, waiting for transfers between devices, shards(): high = lax.ppermute(first_blocks, 'basis', backward)  4.15 us
    all_to_all x1, waiting for transfers between devices, shards(): gathered = lax.all_to_all(sums, 'tile', 0, 0, tiled=True)  3.98 us
    pallas_call x1, Pallas kernels, edges(): pl.pallas_call(edges_kernel, out_shape=(shape, shape), in_specs=[any_spec...  1.35 us
    ppermute x1, starting transfers between devices, shards(): high = lax.ppermute(first_blocks, 'basis', backward)  1.29 us
  transfers between devices with their start and end apart: 3, of which 3 were waited for; matrix products, arithmetic and copies ran while one was open for 1% of the time, Pallas kernels for 18%

commit v1 on v0

--- a/solution.py
+++ b/solution.py
@@ -1,3 +1,5 @@
+import functools
+
 import jax
 import jax.numpy as jnp
 from jax import lax
@@ -81,6 +83,7 @@
 
 
 def inner_kernel(
+    total_blocks,
     first_ref,
     range_ref,
     rot,
@@ -135,7 +138,9 @@
         parts = []
         for d in range(3):
             factor = rot[d, slot] * coupling[d, slot].astype(F32)
-            factor = jnp.where(slot < count, factor, 0.0)
+            target = start + (slot + d - 1)
+            there = (slot < count) & (target >= 0) & (target < total_blocks)
+            factor = jnp.where(there, factor, 0.0)
             parts.append(factor * jnp.dot(turned[d], live, preferred_element_type=F32))
         images[base + (slot - 1)] = (nearer + parts[0]).astype(BF16)
         nearer = further + parts[1]
@@ -154,12 +159,23 @@
         outer[MARGIN + index] = images[MARGIN + blocks + index].T
 
 
-def inner(first, lower_range, rot, coupling, lower_sizes, upper_sizes, lower, upper, dipole):
+def inner(
+    total_blocks,
+    first,
+    lower_range,
+    rot,
+    coupling,
+    lower_sizes,
+    upper_sizes,
+    lower,
+    upper,
+    dipole,
+):
     slots, rows, states = lower.shape
     blocks, _, columns = upper.shape
     small = [in_hbm(a) for a in (lower_range, rot, coupling, lower_sizes, upper_sizes)]
     return pl.pallas_call(
-        inner_kernel,
+        functools.partial(inner_kernel, total_blocks),
         out_shape=(
             pltpu.VMEM((2 * MARGIN, states, rows), BF16),
             pltpu.VMEM((states, columns), F32),
@@ -237,12 +253,13 @@
     tiles = lax.axis_size("tile")
     blocks = upper_vectors.shape[0]
     first = (lax.axis_index("basis") * blocks).astype(jnp.int32).reshape(1)
-    forward = [(i, i + 1) for i in range(parts - 1)]
+    forward = [(i, (i + 1) % parts) for i in range(parts)]
     backward = [(target, source) for source, target in forward]
     last_blocks, first_blocks = edges(upper_sizes, upper_vectors)
     low = lax.ppermute(last_blocks, "basis", forward)
     high = lax.ppermute(first_blocks, "basis", backward)
     images, partial = inner(
+        parts * blocks,
         first,
         lower_range,
         rot_factor.T,

time: 56.3 us -> 52.9 us (0.940)
  blocking collectives: 19.2 us -> 14.9 us
  starting transfers between devices: 13.5 us -> 16.3 us
  waiting for transfers between devices: 8.9 us -> 7.08 us
    ppermute x1, starting transfers between devices: 1.29 us -> 6.22 us  [shards(): high = lax.ppermute(first_blocks, 'basis', backward)]
    all_to_all x1, blocking collectives: 19.2 us -> 14.9 us  [shards(): received = lax.all_to_all(mine, 'basis', 0, 0, tiled=True)]
    ppermute x1, waiting for transfers between devices: 4.15 us -> 0.01 us  [shards(): high = lax.ppermute(first_blocks, 'basis', backward)]
    ppermute x1, waiting for transfers between devices: 0.77 us -> 3.1 us  [shards(): low = lax.ppermute(last_blocks, 'basis', forward)]
    ppermute x1, starting transfers between devices: 4.41 us -> 2.54 us  [shards(): low = lax.ppermute(last_blocks, 'basis', forward)]
  transfers between devices with their start and end apart: 3 -> 3, of which waited for: 3 -> 2; matrix products, arithmetic and copies ran while one was open for 1% -> 1% of each run, Pallas kernels for 18% -> 19%
where the time goes in v1:
time: 52.9 us; the launch traced here: 52.7 us
  starting transfers between devices  16.3 us (31%)
  blocking collectives  14.9 us (28%)
  Pallas kernels  12.7 us (24%)
  waiting for transfers between devices  7.08 us (13%)
  between operations  0.65 us (1%)
  local copies, waits for them, and re-layouts  0.59 us (1%)
  other arithmetic  0.54 us (1%)
    all_to_all x1, blocking collectives, shards(): received = lax.all_to_all(mine, 'basis', 0, 0, tiled=True)  14.9 us
    pallas_call x1, Pallas kernels, inner(): pl.pallas_call(functools.partial(inner_kernel, total_blocks), out_shape=(...  9.86 us
    all_to_all x1, starting transfers between devices, shards(): gathered = lax.all_to_all(sums, 'tile', 0, 0, tiled=True)  7.49 us
    ppermute x1, starting transfers between devices, shards(): high = lax.ppermute(first_blocks, 'basis', backward)  6.22 us
    all_to_all x1, waiting for transfers between devices, shards(): gathered = lax.all_to_all(sums, 'tile', 0, 0, tiled=True)  3.98 us
    ppermute x1, waiting for transfers between devices, shards(): low = lax.ppermute(last_blocks, 'basis', forward)  3.1 us
    ppermute x1, starting transfers between devices, shards(): low = lax.ppermute(last_blocks, 'basis', forward)  2.54 us
    pallas_call x1, Pallas kernels, edges(): pl.pallas_call(edges_kernel, out_shape=(shape, shape), in_specs=[any_spec...  1.35 us
  transfers between devices with their start and end apart: 3, of which 2 were waited for; matrix products, arithmetic and copies ran while one was open for 1% of the time, Pallas kernels for 19%

profile of v1, /device:TPU:1, one launch (start us, length us, event | category | flops | bytes accessed | tf_op | source)
XLA Modules:
  0.0 52.7 jit_solution(15207180765295888231)
XLA Ops:
  0.6 1.4 %edges.1 = (bf16[9,256,128]{2,1,0:T(8,128)(2,1)S(1)}, bf16[9,256,128]{2,1,0:T(8,128)(2,1)S(1)}) custom-call(s32[32]{0:T(128)} %upper_sizes.1, bf16[32,256,128]{2,1,0:T(8,128)(2,1)} %upper_hbm.1), custom_call_target="tpu_custom_call" | custom-call | tf_op jit(solution)/shard_map/edges/pallas_call | solution.py:65
  2.0 2.5 %collective-permute-start = (bf16[9,256,128]{2,1,0:T(8,128)(2,1)S(1)}, bf16[9,256,128]{2,1,0:T(8,128)(2,1)S(1)}, u32[]{:S(2)}, u32[]{:S(2)}) collective-permute-start(bf16[9,256,128]{2,1,0:T(8,128)(2,1)S(1)} %get-tuple-element.8), channel_id=1, source_target_pairs={{0,8},{8,16},{16,24},{24,32},{32,40},{40,48},{48,56},{56,64},{64,7... | collective-permute-start | bytes 1769480 | tf_op jit(solution)/shard_map/ppermute | solution.py:259
  4.5 6.2 %collective-permute-start.1 = (bf16[9,256,128]{2,1,0:T(8,128)(2,1)S(1)}, bf16[9,256,128]{2,1,0:T(8,128)(2,1)S(1)}, u32[]{:S(2)}, u32[]{:S(2)}) collective-permute-start(bf16[9,256,128]{2,1,0:T(8,128)(2,1)S(1)} %get-tuple-element.9), channel_id=1, source_target_pairs={{8,0},{16,8},{24,16},{32,24},{40,32},{48,40},{56,48},{64,56},{72,6... | collective-permute-start | bytes 1769480 | tf_op jit(solution)/shard_map/ppermute | solution.py:260
  10.8 9.9 %inner.1 = (bf16[18,256,256]{2,1,0:T(8,128)(2,1)S(1)}, f32[256,128]{1,0:T(8,128)S(1)}) custom-call(s32[1]{0:T(128)} %bitcast.first_ref, s32[1,2]{1,0:T(1,128)} %range_ref.1, f32[3,48]{1,0:T(4,128)} %bitcast.3, s32[3,48]{1,0:T(4,128)} %bitcast.4, s32[48]{0:T(128)} %lower_sizes.1, s32[32]{0:T(128)} %upper_sizes.1, bf16[48,256,256]{2,1,0:T(8,128)(2,1)} %lower_hbm.1, ...), custom_call_target="tpu_custom_call" | custom-call | tf_op jit(solution)/shard_map/inner/pallas_call | solution.py:177
  20.6 3.1 %collective-permute-done.low = bf16[9,256,128]{2,1,0:T(8,128)(2,1)S(1)} collective-permute-done((bf16[9,256,128]{2,1,0:T(8,128)(2,1)S(1)}, bf16[9,256,128]{2,1,0:T(8,128)(2,1)S(1)}, u32[]{:S(2)}, u32[]{:S(2)}) %collective-permute-start) | collective-permute-done | bytes 589856 | tf_op jit(solution)/shard_map/ppermute | solution.py:259
  23.7 0.0 collective-permute-done.1.high
  23.7 0.8 %outer.1 = bf16[32,8,128]{2,1,0:T(8,128)(2,1)S(1)} custom-call(bf16[9,256,128]{2,1,0:T(8,128)(2,1)S(1)} %collective-permute-done.low, bf16[9,256,128]{2,1,0:T(8,128)(2,1)S(1)} %collective-permute-done.1.high, bf16[18,256,256]{2,1,0:T(8,128)(2,1)S(1)} %get-tuple-element.10.images, f32[256,128]{1,0:T(8,128)S(1)} %get-tuple-element.11.partial), custom_call_target="tpu_custom_call" | custom-call | tf_op jit(solution)/shard_map/outer/pallas_call | solution.py:210
  24.5 14.9 %all_to_all.10.received = bf16[32,8,128]{2,1,0:T(8,128)(2,1)S(1)} all-to-all(bf16[32,8,128]{2,1,0:T(8,128)(2,1)S(1)} %outer.1), channel_id=1, replica_groups=mesh['basis'=32,'tile'=8] {'basis'}, dimensions={0} | all-to-all | bytes 131072 | tf_op jit(solution)/shard_map/all_to_all | solution.py:274
  39.4 0.7 %square.1 = (f32[8,128]{1,0:T(8,128)S(1)}, f32[8,1,8]{2,1,0:T(1,128)}) custom-call(bf16[32,8,128]{2,1,0:T(8,128)(2,1)S(1)} %all_to_all.10.received), custom_call_target="tpu_custom_call" | custom-call | tf_op jit(solution)/shard_map/square/pallas_call | solution.py:230
  40.1 7.5 %all-to-all-start.1 = ((f32[8,1,8]{2,1,0:T(1,128)}), f32[8,1,8]{2,1,0:T(1,128)S(1)}, u32[]{:S(2)}, u32[]{:S(2)}) async-start(f32[8,1,8]{2,1,0:T(1,128)} %get-tuple-element.13), calls=%async_computation.1 | async-start | bytes 8192 | tf_op jit(solution)/shard_map/all_to_all | solution.py:276
  47.6 0.6 %copy.10 = f32[8,128]{1,0:T(8,128)} copy(f32[8,128]{1,0:T(8,128)S(1)} %get-tuple-element.14) | data formatting | bytes 8192
  48.2 4.0 %all-to-all-done.1 = f32[8,1,8]{2,1,0:T(1,128)S(1)} async-done(((f32[8,1,8]{2,1,0:T(1,128)}), f32[8,1,8]{2,1,0:T(1,128)S(1)}, u32[]{:S(2)}, u32[]{:S(2)}) %all-to-all-start.1) | async-done | bytes 288 | tf_op jit(solution)/shard_map/all_to_all | solution.py:276
  52.2 0.5 %reduce_sum.9 = f32[8]{0:T(128)} reduce(f32[8,1,8]{2,1,0:T(1,128)S(1)} %all-to-all-done.1, f32[]{:T(128)} %constant.9.clone.1), dimensions={0,1}, to_apply=%region_0.0 | reduce | flops 56 | bytes 292 | tf_op jit(solution)/shard_map/reduce_sum | solution.py:277
Async XLA Ops:
  2.0 21.7 %collective-permute-start = (bf16[9,256,128]{2,1,0:T(8,128)(2,1)S(1)}, bf16[9,256,128]{2,1,0:T(8,128)(2,1)S(1)}, u32[]{:S(2)}, u32[]{:S(2)}) collective-permute-start(bf16[9,256,128]{2,1,0:T(8,128)(2,1)S(1)} %get-tuple-element.8), channel_id=1, source_target_pairs={{0,8},{8,16},{16,24},{24,32},{32,40},{40,48},{48,56},{56,64},{64,7... | collective-permute-start | bytes 1769480 | tf_op jit(solution)/shard_map/ppermute | solution.py:259
  4.5 19.2 %collective-permute-start.1 = (bf16[9,256,128]{2,1,0:T(8,128)(2,1)S(1)}, bf16[9,256,128]{2,1,0:T(8,128)(2,1)S(1)}, u32[]{:S(2)}, u32[]{:S(2)}) collective-permute-start(bf16[9,256,128]{2,1,0:T(8,128)(2,1)S(1)} %get-tuple-element.9), channel_id=1, source_target_pairs={{8,0},{16,8},{24,16},{32,24},{40,32},{48,40},{56,48},{64,56},{72,6... | collective-permute-start | bytes 1769480 | tf_op jit(solution)/shard_map/ppermute | solution.py:260
  40.1 12.1 %all-to-all-start.1 = ((f32[8,1,8]{2,1,0:T(1,128)}), f32[8,1,8]{2,1,0:T(1,128)S(1)}, u32[]{:S(2)}, u32[]{:S(2)}) async-start(f32[8,1,8]{2,1,0:T(1,128)} %get-tuple-element.13), calls=%async_computation.1 | async-start | bytes 8192 | tf_op jit(solution)/shard_map/all_to_all | solution.py:276

commit v2 on v1

--- a/solution.py
+++ b/solution.py
@@ -93,7 +93,8 @@
     lower_hbm,
     upper_hbm,
     dipole_hbm,
-    outer,
+    above,
+    below,
     partial,
     images,
     turned,
@@ -155,8 +156,8 @@
         total += jnp.dot(live.T, images[MARGIN + block], preferred_element_type=F32)
     partial[...] = total.T
     for index in range(MARGIN):
-        outer[index] = images[index].T
-        outer[MARGIN + index] = images[MARGIN + blocks + index].T
+        below[index] = images[index].T
+        above[index] = images[MARGIN + blocks + index].T
 
 
 def inner(
@@ -177,11 +178,12 @@
     return pl.pallas_call(
         functools.partial(inner_kernel, total_blocks),
         out_shape=(
-            pltpu.VMEM((2 * MARGIN, states, rows), BF16),
+            pltpu.VMEM((MARGIN, states, rows), BF16),
+            pltpu.VMEM((MARGIN, states, rows), BF16),
             pltpu.VMEM((states, columns), F32),
         ),
         in_specs=[smem_spec() for _ in range(6)] + [any_spec() for _ in range(3)],
-        out_specs=(vmem_spec(), vmem_spec()),
+        out_specs=(vmem_spec(), vmem_spec(), vmem_spec()),
         scratch_shapes=[
             pltpu.VMEM((slots + 2 * MARGIN + 2, rows, states), BF16),
             pltpu.VMEM((3, rows, rows), BF16),
@@ -195,26 +197,22 @@
     )(first, *small, in_hbm(lower), in_hbm(upper), in_hbm(dipole))
 
 
-def outer_kernel(low, high, images, partial, out):
+def outer_kernel(halo, images, partial, out):
     total = partial[...]
-    margin = low.shape[0]
-    for index in range(margin):
-        total += jnp.dot(images[index], low[index], preferred_element_type=F32)
-    for index in range(margin):
-        total += jnp.dot(images[margin + index], high[index], preferred_element_type=F32)
+    for index in range(halo.shape[0]):
+        total += jnp.dot(images[index], halo[index], preferred_element_type=F32)
     out[...] = total.reshape(out.shape).astype(out.dtype)
 
 
-def outer(low, high, images, partial, parts):
-    states, columns = partial.shape
+def outer(halo, images, partial, shape, dtype):
     return pl.pallas_call(
         outer_kernel,
-        out_shape=pltpu.VMEM((parts, states // parts, columns), BF16),
-        in_specs=[vmem_spec() for _ in range(4)],
+        out_shape=pltpu.VMEM(shape, dtype),
+        in_specs=[vmem_spec() for _ in range(3)],
         out_specs=vmem_spec(),
         compiler_params=pltpu.CompilerParams(vmem_limit_bytes=VMEM_BYTES),
         name="outer",
-    )(in_vmem(low), in_vmem(high), images, partial)
+    )(in_vmem(halo), images, partial)
 
 
 def square_kernel(received, strength, sums):
@@ -222,16 +220,16 @@
     squared = moment * moment
     strength[...] = squared
     row = jnp.sum(squared.T, axis=0, keepdims=True) * (1.0 / NUP)
-    sums[...] = jnp.broadcast_to(row[None], sums.shape)
-
-
-def square(received, tiles):
+    sums[...] = row
+
+
+def square(received):
     _, band, columns = received.shape
     return pl.pallas_call(
         square_kernel,
         out_shape=(
             pltpu.VMEM((band, columns), F32),
-            pltpu.VMEM((tiles, 1, band), F32),
+            pltpu.VMEM((1, band), F32),
         ),
         in_specs=[vmem_spec()],
         out_specs=(vmem_spec(), vmem_spec()),
@@ -258,7 +256,7 @@
     last_blocks, first_blocks = edges(upper_sizes, upper_vectors)
     low = lax.ppermute(last_blocks, "basis", forward)
     high = lax.ppermute(first_blocks, "basis", backward)
-    images, partial = inner(
+    above, below, partial = inner(
         parts * blocks,
         first,
         lower_range,
@@ -270,11 +268,17 @@
         upper_vectors,
         dipole_vib,
     )
-    mine = outer(low, high, images, partial, parts)
+    partial = outer(low, below, partial, partial.shape, F32)
+    states, columns = partial.shape
+    mine = outer(high, above, partial, (parts, states // parts, columns), BF16)
     received = lax.all_to_all(mine, "basis", 0, 0, tiled=True)
-    strength, sums = square(received, tiles)
-    gathered = lax.all_to_all(sums, "tile", 0, 0, tiled=True)
-    average = jnp.sum(gathered[:, 0, :], axis=0)
+    strength, sums = square(received)
+    sums = sums + lax.ppermute(sums, "tile", [(i, i ^ 1) for i in range(tiles)])
+    others = [
+        lax.ppermute(sums, "tile", [(i, (i + step) % tiles) for i in range(tiles)])
+        for step in range(2, tiles, 2)
+    ]
+    average = ((others[0] + others[2]) + (sums + others[1]))[0]
     return (strength, average)
 
 

time: 52.9 us -> 51.6 us (0.975)
    all_to_all x1 -> x0, starting transfers between devices: 7.49 us -> none  [shards(): gathered = lax.all_to_all(sums, 'tile', 0, 0, tiled=True)]
    ppermute x0 -> x4, starting transfers between devices: none -> 7.4 us  [the longest x3 4.38 us: shards(): lax.ppermute(sums, 'tile', [(i, (i + step) % tiles) for i in range(tiles)])]
    all_to_all x1 -> x0, waiting for transfers between devices: 3.98 us -> none  [shards(): gathered = lax.all_to_all(sums, 'tile', 0, 0, tiled=True)]
    ppermute x0 -> x4, waiting for transfers between devices: none -> 3.73 us  [the longest x3 2.91 us: shards(): lax.ppermute(sums, 'tile', [(i, (i + step) % tiles) for i in range(tiles)])]
    pallas_call x1, Pallas kernels: 0.74 us -> 0.14 us  [square(): pl.pallas_call(square_kernel, out_shape=(pltpu.VMEM((band, columns), F32)...]
    reduce_sum x1 -> x0, other arithmetic: 0.54 us -> none  [shards(): average = jnp.sum(gathered[:, 0, :], axis=0)]
  transfers between devices with their start and end apart: 3 -> 6, of which waited for: 2 -> 4; matrix products, arithmetic and copies ran while one was open for 1% -> 0% of each run, Pallas kernels for 19% -> 20%
where the time goes in v2:
time: 51.6 us; the launch traced here: 51.5 us
  starting transfers between devices  16.2 us (31%)
  blocking collectives  14.4 us (28%)
  Pallas kernels  12.3 us (24%)
  waiting for transfers between devices  6.83 us (13%)
  between operations  0.67 us (1%)
  local copies, waits for them, and re-layouts  0.59 us (1%)
  other arithmetic  0.52 us (1%)
    all_to_all x1, blocking collectives, shards(): received = lax.all_to_all(mine, 'basis', 0, 0, tiled=True)  14.4 us
    pallas_call x1, Pallas kernels, inner(): pl.pallas_call(functools.partial(inner_kernel, total_blocks), out_shape=(...  9.86 us
    ppermute x1, starting transfers between devices, shards(): high = lax.ppermute(first_blocks, 'basis', backward)  6.22 us
    ppermute x3, starting transfers between devices, shards(): lax.ppermute(sums, 'tile', [(i, (i + step) % tiles) for i in range(tiles)])  4.38 us
    ppermute x1, waiting for transfers between devices, shards(): low = lax.ppermute(last_blocks, 'basis', forward)  3.1 us
    ppermute x1, starting transfers between devices, shards(): sums = sums + lax.ppermute(sums, 'tile', [(i, i ^ 1) for i in range(tiles)])  3.02 us
    ppermute x3, waiting for transfers between devices, shards(): lax.ppermute(sums, 'tile', [(i, (i + step) % tiles) for i in range(tiles)])  2.91 us
    ppermute x1, starting transfers between devices, shards(): low = lax.ppermute(last_blocks, 'basis', forward)  2.54 us
  transfers between devices with their start and end apart: 6, of which 4 were waited for; matrix products, arithmetic and copies ran while one was open for 0% of the time, Pallas kernels for 20%

profile of v2, /device:TPU:1, one launch (start us, length us, event | category | flops | bytes accessed | tf_op | source)
XLA Modules:
  0.0 51.5 jit_solution(15155216457595183908)
XLA Ops:
  0.6 1.4 %edges.1 = (bf16[9,256,128]{2,1,0:T(8,128)(2,1)S(1)}, bf16[9,256,128]{2,1,0:T(8,128)(2,1)S(1)}) custom-call(s32[32]{0:T(128)} %upper_sizes.1, bf16[32,256,128]{2,1,0:T(8,128)(2,1)} %upper_hbm.1), custom_call_target="tpu_custom_call" | custom-call | tf_op jit(solution)/shard_map/edges/pallas_call | solution.py:65
  2.0 2.5 %collective-permute-start.1 = (bf16[9,256,128]{2,1,0:T(8,128)(2,1)S(1)}, bf16[9,256,128]{2,1,0:T(8,128)(2,1)S(1)}, u32[]{:S(2)}, u32[]{:S(2)}) collective-permute-start(bf16[9,256,128]{2,1,0:T(8,128)(2,1)S(1)} %get-tuple-element.11), channel_id=1, source_target_pairs={{0,8},{8,16},{16,24},{24,32},{32,40},{40,48},{48,56},{56,64},{64,7... | collective-permute-start | bytes 1769480 | tf_op jit(solution)/shard_map/ppermute | solution.py:257
  4.5 6.2 %collective-permute-start = (bf16[9,256,128]{2,1,0:T(8,128)(2,1)S(1)}, bf16[9,256,128]{2,1,0:T(8,128)(2,1)S(1)}, u32[]{:S(2)}, u32[]{:S(2)}) collective-permute-start(bf16[9,256,128]{2,1,0:T(8,128)(2,1)S(1)} %get-tuple-element.9), channel_id=1, source_target_pairs={{8,0},{16,8},{24,16},{32,24},{40,32},{48,40},{56,48},{64,56},{72,6... | collective-permute-start | bytes 1769480 | tf_op jit(solution)/shard_map/ppermute | solution.py:258
  10.8 9.9 %inner.1 = (bf16[9,256,256]{2,1,0:T(8,128)(2,1)S(1)}, bf16[9,256,256]{2,1,0:T(8,128)(2,1)S(1)}, f32[256,128]{1,0:T(8,128)S(1)}) custom-call(s32[1]{0:T(128)} %bitcast.first_ref, s32[1,2]{1,0:T(1,128)} %range_ref.1, f32[3,48]{1,0:T(4,128)} %bitcast.5, s32[3,48]{1,0:T(4,128)} %bitcast.6, s32[48]{0:T(128)} %lower_sizes.1, s32[32]{0:T(128)} %upper_sizes.1, ...), custom_call_target="tpu_custom_call" | custom-call | tf_op jit(solution)/shard_map/inner/pallas_call | solution.py:178
  20.6 3.1 %collective-permute-done.1.halo = bf16[9,256,128]{2,1,0:T(8,128)(2,1)S(1)} collective-permute-done((bf16[9,256,128]{2,1,0:T(8,128)(2,1)S(1)}, bf16[9,256,128]{2,1,0:T(8,128)(2,1)S(1)}, u32[]{:S(2)}, u32[]{:S(2)}) %collective-permute-start.1) | collective-permute-done | bytes 589856 | tf_op jit(solution)/shard_map/ppermute | solution.py:257
  23.7 0.5 outer.2.partial
  24.2 0.0 collective-permute-done.halo
  24.2 0.5 outer.3
  24.7 14.4 %all_to_all.5.received = bf16[32,8,128]{2,1,0:T(8,128)(2,1)S(1)} all-to-all(bf16[32,8,128]{2,1,0:T(8,128)(2,1)S(1)} %outer.3), channel_id=1, replica_groups=mesh['basis'=32,'tile'=8] {'basis'}, dimensions={0} | all-to-all | bytes 131072 | tf_op jit(solution)/shard_map/all_to_all | solution.py:274
  39.1 0.1 square.1
  39.2 0.6 %copy.10 = f32[8,128]{1,0:T(8,128)} copy(f32[8,128]{1,0:T(8,128)S(1)} %get-tuple-element.16) | data formatting | bytes 8192
  39.8 3.0 %collective-permute-start.2 = (f32[1,8]{1,0:T(1,128)S(1)}, f32[1,8]{1,0:T(1,128)S(1)}, u32[]{:S(2)}, u32[]{:S(2)}) collective-permute-start(f32[1,8]{1,0:T(1,128)S(1)} %get-tuple-element.15), channel_id=1, source_target_pairs={{0,1},{1,0},{2,3},{3,2},{4,5},{5,4},{6,7},{7,6},{8,9},{9,8},{10,11... | collective-permute-start | bytes 104 | tf_op jit(solution)/shard_map/ppermute | solution.py:276
  42.8 0.8 %collective-permute-done.2 = f32[1,8]{1,0:T(1,128)S(1)} collective-permute-done((f32[1,8]{1,0:T(1,128)S(1)}, f32[1,8]{1,0:T(1,128)S(1)}, u32[]{:S(2)}, u32[]{:S(2)}) %collective-permute-start.2) | collective-permute-done | bytes 64 | tf_op jit(solution)/shard_map/ppermute | solution.py:276
  43.6 2.9 %collective-permute-start.5 = (f32[1,8]{1,0:T(1,128)S(1)}, f32[1,8]{1,0:T(1,128)S(1)}, u32[]{:S(2)}, u32[]{:S(2)}) collective-permute-start(f32[1,8]{1,0:T(1,128)S(1)} %add.12), channel_id=1, source_target_pairs={{0,4},{1,5},{2,6},{3,7},{4,0},{5,1},{6,2},{7,3},{8,12},{9,13},{10,... | collective-permute-start | bytes 104 | tf_op jit(solution)/shard_map/ppermute | solution.py:278
  46.6 0.8 %collective-permute-start.4 = (f32[1,8]{1,0:T(1,128)S(1)}, f32[1,8]{1,0:T(1,128)S(1)}, u32[]{:S(2)}, u32[]{:S(2)}) collective-permute-start(f32[1,8]{1,0:T(1,128)S(1)} %add.12), channel_id=1, source_target_pairs={{0,6},{1,7},{2,0},{3,1},{4,2},{5,3},{6,4},{7,5},{8,14},{9,15},{10,... | collective-permute-start | bytes 104 | tf_op jit(solution)/shard_map/ppermute | solution.py:278
  47.3 0.7 %collective-permute-start.3 = (f32[1,8]{1,0:T(1,128)S(1)}, f32[1,8]{1,0:T(1,128)S(1)}, u32[]{:S(2)}, u32[]{:S(2)}) collective-permute-start(f32[1,8]{1,0:T(1,128)S(1)} %add.12), channel_id=1, source_target_pairs={{0,2},{1,3},{2,4},{3,5},{4,6},{5,7},{6,0},{7,1},{8,10},{9,11},{10,... | collective-permute-start | bytes 104 | tf_op jit(solution)/shard_map/ppermute | solution.py:278
  48.0 0.0 collective-permute-done.5
  48.0 0.9 %collective-permute-done.4 = f32[1,8]{1,0:T(1,128)S(1)} collective-permute-done((f32[1,8]{1,0:T(1,128)S(1)}, f32[1,8]{1,0:T(1,128)S(1)}, u32[]{:S(2)}, u32[]{:S(2)}) %collective-permute-start.4) | collective-permute-done | bytes 64 | tf_op jit(solution)/shard_map/ppermute | solution.py:278
  49.0 2.0 %collective-permute-done.3 = f32[1,8]{1,0:T(1,128)S(1)} collective-permute-done((f32[1,8]{1,0:T(1,128)S(1)}, f32[1,8]{1,0:T(1,128)S(1)}, u32[]{:S(2)}, u32[]{:S(2)}) %collective-permute-start.3) | collective-permute-done | bytes 64 | tf_op jit(solution)/shard_map/ppermute | solution.py:278
  50.9 0.5 %add_bitcast_fusion = f32[8]{0:T(128)} fusion(f32[1,8]{1,0:T(1,128)S(1)} %add.12, f32[1,8]{1,0:T(1,128)S(1)} %collective-permute-done.5, f32[1,8]{1,0:T(1,128)S(1)} %collective-permute-done.3, f32[1,8]{1,0:T(1,128)S(1)} %collective-permute-done.4), kind=kLoop, calls=%fused_computation | loop fusion | flops 24 | bytes 160 | tf_op jit(solution)/shard_map/squeeze | solution.py:281
  (1 shorter events, 0.0 us)
Async XLA Ops:
  2.0 21.7 %collective-permute-start.1 = (bf16[9,256,128]{2,1,0:T(8,128)(2,1)S(1)}, bf16[9,256,128]{2,1,0:T(8,128)(2,1)S(1)}, u32[]{:S(2)}, u32[]{:S(2)}) collective-permute-start(bf16[9,256,128]{2,1,0:T(8,128)(2,1)S(1)} %get-tuple-element.11), channel_id=1, source_target_pairs={{0,8},{8,16},{16,24},{24,32},{32,40},{40,48},{48,56},{56,64},{64,7... | collective-permute-start | bytes 1769480 | tf_op jit(solution)/shard_map/ppermute | solution.py:257
  4.5 19.7 %collective-permute-start = (bf16[9,256,128]{2,1,0:T(8,128)(2,1)S(1)}, bf16[9,256,128]{2,1,0:T(8,128)(2,1)S(1)}, u32[]{:S(2)}, u32[]{:S(2)}) collective-permute-start(bf16[9,256,128]{2,1,0:T(8,128)(2,1)S(1)} %get-tuple-element.9), channel_id=1, source_target_pairs={{8,0},{16,8},{24,16},{32,24},{40,32},{48,40},{56,48},{64,56},{72,6... | collective-permute-start | bytes 1769480 | tf_op jit(solution)/shard_map/ppermute | solution.py:258
  39.8 3.8 %collective-permute-start.2 = (f32[1,8]{1,0:T(1,128)S(1)}, f32[1,8]{1,0:T(1,128)S(1)}, u32[]{:S(2)}, u32[]{:S(2)}) collective-permute-start(f32[1,8]{1,0:T(1,128)S(1)} %get-tuple-element.15), channel_id=1, source_target_pairs={{0,1},{1,0},{2,3},{3,2},{4,5},{5,4},{6,7},{7,6},{8,9},{9,8},{10,11... | collective-permute-start | bytes 104 | tf_op jit(solution)/shard_map/ppermute | solution.py:276
  43.6 4.4 %collective-permute-start.5 = (f32[1,8]{1,0:T(1,128)S(1)}, f32[1,8]{1,0:T(1,128)S(1)}, u32[]{:S(2)}, u32[]{:S(2)}) collective-permute-start(f32[1,8]{1,0:T(1,128)S(1)} %add.12), channel_id=1, source_target_pairs={{0,4},{1,5},{2,6},{3,7},{4,0},{5,1},{6,2},{7,3},{8,12},{9,13},{10,... | collective-permute-start | bytes 104 | tf_op jit(solution)/shard_map/ppermute | solution.py:278
  46.6 2.4 %collective-permute-start.4 = (f32[1,8]{1,0:T(1,128)S(1)}, f32[1,8]{1,0:T(1,128)S(1)}, u32[]{:S(2)}, u32[]{:S(2)}) collective-permute-start(f32[1,8]{1,0:T(1,128)S(1)} %add.12), channel_id=1, source_target_pairs={{0,6},{1,7},{2,0},{3,1},{4,2},{5,3},{6,4},{7,5},{8,14},{9,15},{10,... | collective-permute-start | bytes 104 | tf_op jit(solution)/shard_map/ppermute | solution.py:278
  47.3 3.6 %collective-permute-start.3 = (f32[1,8]{1,0:T(1,128)S(1)}, f32[1,8]{1,0:T(1,128)S(1)}, u32[]{:S(2)}, u32[]{:S(2)}) collective-permute-start(f32[1,8]{1,0:T(1,128)S(1)} %add.12), channel_id=1, source_target_pairs={{0,2},{1,3},{2,4},{3,5},{4,6},{5,7},{6,0},{7,1},{8,10},{9,11},{10,... | collective-permute-start | bytes 104 | tf_op jit(solution)/shard_map/ppermute | solution.py:278

commit v3 on v2

--- a/solution.py
+++ b/solution.py
@@ -38,12 +38,20 @@
     return pltpu.with_memory_space_constraint(array, pltpu.VMEM)
 
 
-def edges_kernel(sizes_hbm, upper, low, high, sizes, sems):
+def even():
+    return lax.rem(lax.axis_index("basis"), 2) == 0
+
+
+def edges_kernel(sizes_hbm, upper, inward, outward, sizes, sems):
     blocks, rows, columns = upper.shape
-    margin = low.shape[0]
+    margin = inward.shape[0]
+    firsts = [
+        jnp.where(even(), blocks - margin, 0),
+        jnp.where(even(), 0, blocks - margin),
+    ]
     copies = [
-        pltpu.make_async_copy(upper.at[pl.ds(blocks - margin, margin)], low, sems.at[0]),
-        pltpu.make_async_copy(upper.at[pl.ds(0, margin)], high, sems.at[1]),
+        pltpu.make_async_copy(upper.at[pl.ds(first, margin)], out, sems.at[index])
+        for index, (first, out) in enumerate(zip(firsts, (inward, outward)))
     ]
     known = pltpu.make_async_copy(sizes_hbm, sizes, sems.at[2])
     known.start()
@@ -51,7 +59,7 @@
         copy.start()
     row_ids = LEAST + lax.broadcasted_iota(jnp.int32, (rows - LEAST, columns), 0)
     known.wait()
-    for copy, out, first in zip(copies, (low, high), (blocks - margin, 0)):
+    for copy, out, first in zip(copies, (inward, outward), firsts):
         copy.wait()
         for block in range(margin):
             out[block, LEAST:] = jnp.where(
@@ -84,7 +92,6 @@
 
 def inner_kernel(
     total_blocks,
-    first_ref,
     range_ref,
     rot,
     coupling,
@@ -93,8 +100,8 @@
     lower_hbm,
     upper_hbm,
     dipole_hbm,
-    above,
-    below,
+    inward,
+    outward,
     partial,
     images,
     turned,
@@ -107,7 +114,7 @@
     blocks, _, columns = upper.shape
     start = range_ref[0, 0]
     count = range_ref[0, 1] - start
-    base = start - first_ref[0] + MARGIN
+    base = start - lax.axis_index("basis") * blocks + MARGIN
     chunks = slots // CHUNK
     copies = [
         pltpu.make_async_copy(
@@ -155,14 +162,14 @@
         live = masked(upper[block], upper_sizes[block])
         total += jnp.dot(live.T, images[MARGIN + block], preferred_element_type=F32)
     partial[...] = total.T
+    low, high = 0, MARGIN + blocks
     for index in range(MARGIN):
-        below[index] = images[index].T
-        above[index] = images[MARGIN + blocks + index].T
+        inward[index] = images[jnp.where(even(), high, low) + index].T
+        outward[index] = images[jnp.where(even(), low, high) + index].T
 
 
 def inner(
     total_blocks,
-    first,
     lower_range,
     rot,
     coupling,
@@ -182,7 +189,7 @@
             pltpu.VMEM((MARGIN, states, rows), BF16),
             pltpu.VMEM((states, columns), F32),
         ),
-        in_specs=[smem_spec() for _ in range(6)] + [any_spec() for _ in range(3)],
+        in_specs=[smem_spec() for _ in range(5)] + [any_spec() for _ in range(3)],
         out_specs=(vmem_spec(), vmem_spec(), vmem_spec()),
         scratch_shapes=[
             pltpu.VMEM((slots + 2 * MARGIN + 2, rows, states), BF16),
@@ -194,7 +201,7 @@
         ],
         compiler_params=pltpu.CompilerParams(vmem_limit_bytes=VMEM_BYTES),
         name="inner",
-    )(first, *small, in_hbm(lower), in_hbm(upper), in_hbm(dipole))
+    )(*small, in_hbm(lower), in_hbm(upper), in_hbm(dipole))
 
 
 def outer_kernel(halo, images, partial, out):
@@ -228,7 +235,7 @@
     return pl.pallas_call(
         square_kernel,
         out_shape=(
-            pltpu.VMEM((band, columns), F32),
+            jax.ShapeDtypeStruct((band, columns), F32),
             pltpu.VMEM((1, band), F32),
         ),
         in_specs=[vmem_spec()],
@@ -250,15 +257,18 @@
     parts = lax.axis_size("basis")
     tiles = lax.axis_size("tile")
     blocks = upper_vectors.shape[0]
-    first = (lax.axis_index("basis") * blocks).astype(jnp.int32).reshape(1)
-    forward = [(i, (i + 1) % parts) for i in range(parts)]
-    backward = [(target, source) for source, target in forward]
-    last_blocks, first_blocks = edges(upper_sizes, upper_vectors)
-    low = lax.ppermute(last_blocks, "basis", forward)
-    high = lax.ppermute(first_blocks, "basis", backward)
-    above, below, partial = inner(
+    pairs = [(i, i ^ 1) for i in range(parts)]
+    others = []
+    for i in range(parts):
+        other = ((i + 1) ^ 1) - 1
+        for tile in range(tiles):
+            there = (other, tile) if 0 <= other < parts else (i, tile ^ 1)
+            others.append((i * tiles + tile, there[0] * tiles + there[1]))
+    inward_blocks, outward_blocks = edges(upper_sizes, upper_vectors)
+    inward_halo = lax.ppermute(inward_blocks, "basis", pairs)
+    outward_halo = lax.ppermute(outward_blocks, ("basis", "tile"), others)
+    inward, outward, partial = inner(
         parts * blocks,
-        first,
         lower_range,
         rot_factor.T,
         coupling.T,
@@ -268,9 +278,9 @@
         upper_vectors,
         dipole_vib,
     )
-    partial = outer(low, below, partial, partial.shape, F32)
+    partial = outer(inward_halo, inward, partial, partial.shape, F32)
     states, columns = partial.shape
-    mine = outer(high, above, partial, (parts, states // parts, columns), BF16)
+    mine = outer(outward_halo, outward, partial, (parts, states // parts, columns), BF16)
     received = lax.all_to_all(mine, "basis", 0, 0, tiled=True)
     strength, sums = square(received)
     sums = sums + lax.ppermute(sums, "tile", [(i, i ^ 1) for i in range(tiles)])

time: 51.6 us -> 51.6 us (level)
  blocking collectives: 14.4 us -> 21.4 us
  starting transfers between devices: 16.2 us -> 11.2 us
  waiting for transfers between devices: 6.83 us -> 4.9 us
  local copies, waits for them, and re-layouts: 0.59 us -> 0 us
    all_to_all x1, blocking collectives: 14.4 us -> 21.4 us  [shards(): received = lax.all_to_all(mine, 'basis', 0, 0, tiled=True)]
    ppermute x2, starting transfers between devices: 8.77 us -> 3.51 us  [the longest x1 2.55 us: shards(): inward_halo = lax.ppermute(inward_blocks, 'basis', pairs)]
    ppermute x2, waiting for transfers between devices: 3.1 us -> 1.18 us  [the longest x1 1.17 us: shards(): inward_halo = lax.ppermute(inward_blocks, 'basis', pairs)]
    unnamed x1 -> x0, local copies, waits for them, and re-layouts: 0.59 us -> none
where the time goes in v3:
time: 51.6 us; the launch traced here: 51.5 us
  blocking collectives  21.4 us (41%)
  Pallas kernels  12.8 us (25%)
  starting transfers between devices  11.2 us (22%)
  waiting for transfers between devices  4.9 us (9%)
  between operations  0.67 us (1%)
  other arithmetic  0.52 us (1%)
    all_to_all x1, blocking collectives, shards(): received = lax.all_to_all(mine, 'basis', 0, 0, tiled=True)  21.4 us
    pallas_call x1, Pallas kernels, inner(): pl.pallas_call(functools.partial(inner_kernel, total_blocks), out_shape=(...  9.86 us
    ppermute x3, starting transfers between devices, shards(): lax.ppermute(sums, 'tile', [(i, (i + step) % tiles) for i in range(tiles)])  4.38 us
    ppermute x1, starting transfers between devices, shards(): sums = sums + lax.ppermute(sums, 'tile', [(i, i ^ 1) for i in range(tiles)])  3.28 us
    ppermute x3, waiting for transfers between devices, shards(): lax.ppermute(sums, 'tile', [(i, (i + step) % tiles) for i in range(tiles)])  2.91 us
    ppermute x1, starting transfers between devices, shards(): inward_halo = lax.ppermute(inward_blocks, 'basis', pairs)  2.55 us
    pallas_call x1, Pallas kernels, edges(): pl.pallas_call(edges_kernel, out_shape=(shape, shape), in_specs=[any_spec...  1.37 us
    ppermute x1, waiting for transfers between devices, shards(): inward_halo = lax.ppermute(inward_blocks, 'basis', pairs)  1.17 us
  transfers between devices with their start and end apart: 6, of which 4 were waited for; matrix products, arithmetic and copies ran while one was open for 0% of the time, Pallas kernels for 20%

profile of v3, /device:TPU:1, one launch (start us, length us, event | category | flops | bytes accessed | tf_op | source)
XLA Modules:
  0.0 51.5 jit_solution(14632405965403957664)
XLA Ops:
  0.6 1.4 %edges.1 = (bf16[9,256,128]{2,1,0:T(8,128)(2,1)S(1)}, bf16[9,256,128]{2,1,0:T(8,128)(2,1)S(1)}) custom-call(s32[32]{0:T(128)} %upper_sizes.1, bf16[32,256,128]{2,1,0:T(8,128)(2,1)} %upper_hbm.1), custom_call_target="tpu_custom_call" | custom-call | tf_op jit(solution)/shard_map/edges/pallas_call | solution.py:73
  2.0 2.6 %collective-permute-start.1 = (bf16[9,256,128]{2,1,0:T(8,128)(2,1)S(1)}, bf16[9,256,128]{2,1,0:T(8,128)(2,1)S(1)}, u32[]{:S(2)}, u32[]{:S(2)}) collective-permute-start(bf16[9,256,128]{2,1,0:T(8,128)(2,1)S(1)} %get-tuple-element.11), channel_id=1, source_target_pairs={{0,8},{8,0},{16,24},{24,16},{32,40},{40,32},{48,56},{56,48},{64,72... | collective-permute-start | bytes 1769480 | tf_op jit(solution)/shard_map/ppermute | solution.py:268
  4.6 1.0 %collective-permute-start = (bf16[9,256,128]{2,1,0:T(8,128)(2,1)S(1)}, bf16[9,256,128]{2,1,0:T(8,128)(2,1)S(1)}, u32[]{:S(2)}, u32[]{:S(2)}) collective-permute-start(bf16[9,256,128]{2,1,0:T(8,128)(2,1)S(1)} %get-tuple-element.9), channel_id=1, source_target_pairs={{0,1},{1,0},{2,3},{3,2},{4,5},{5,4},{6,7},{7,6},{8,16},{9,17},{10,... | collective-permute-start | bytes 1769480 | tf_op jit(solution)/shard_map/ppermute | solution.py:269
  5.5 9.9 %inner.1 = (bf16[9,256,256]{2,1,0:T(8,128)(2,1)S(1)}, bf16[9,256,256]{2,1,0:T(8,128)(2,1)S(1)}, f32[256,128]{1,0:T(8,128)S(1)}) custom-call(s32[1,2]{1,0:T(1,128)} %range_ref.1, f32[3,48]{1,0:T(4,128)} %bitcast.4, s32[3,48]{1,0:T(4,128)} %bitcast.5, s32[48]{0:T(128)} %lower_sizes.1, s32[32]{0:T(128)} %upper_sizes.1, bf16[48,256,256]{2,1,0:T(8,128)(2,1)} %lower_hbm.1, ...), custom_call_target="tpu_custom_call" | custom-call | tf_op jit(solution)/shard_map/inner/pallas_call | solution.py:185
  15.4 1.2 %collective-permute-done.1.halo = bf16[9,256,128]{2,1,0:T(8,128)(2,1)S(1)} collective-permute-done((bf16[9,256,128]{2,1,0:T(8,128)(2,1)S(1)}, bf16[9,256,128]{2,1,0:T(8,128)(2,1)S(1)}, u32[]{:S(2)}, u32[]{:S(2)}) %collective-permute-start.1) | collective-permute-done | bytes 589856 | tf_op jit(solution)/shard_map/ppermute | solution.py:268
  16.6 0.5 outer.2.partial
  17.0 0.0 collective-permute-done.halo
  17.0 0.5 outer.3
  17.5 21.4 %all_to_all.5.received = bf16[32,8,128]{2,1,0:T(8,128)(2,1)S(1)} all-to-all(bf16[32,8,128]{2,1,0:T(8,128)(2,1)S(1)} %outer.3), channel_id=1, replica_groups=mesh['basis'=32,'tile'=8] {'basis'}, dimensions={0} | all-to-all | bytes 131072 | tf_op jit(solution)/shard_map/all_to_all | solution.py:284
  38.9 0.6 %square.1 = (f32[8,128]{1,0:T(8,128)}, f32[1,8]{1,0:T(1,128)S(1)}) custom-call(bf16[32,8,128]{2,1,0:T(8,128)(2,1)S(1)} %all_to_all.5.received), custom_call_target="tpu_custom_call" | custom-call | tf_op jit(solution)/shard_map/square/pallas_call | solution.py:235
  39.5 3.3 %collective-permute-start.2 = (f32[1,8]{1,0:T(1,128)S(1)}, f32[1,8]{1,0:T(1,128)S(1)}, u32[]{:S(2)}, u32[]{:S(2)}) collective-permute-start(f32[1,8]{1,0:T(1,128)S(1)} %get-tuple-element.15), channel_id=1, source_target_pairs={{0,1},{1,0},{2,3},{3,2},{4,5},{5,4},{6,7},{7,6},{8,9},{9,8},{10,11... | collective-permute-start | bytes 104 | tf_op jit(solution)/shard_map/ppermute | solution.py:286
  42.8 0.8 %collective-permute-done.2 = f32[1,8]{1,0:T(1,128)S(1)} collective-permute-done((f32[1,8]{1,0:T(1,128)S(1)}, f32[1,8]{1,0:T(1,128)S(1)}, u32[]{:S(2)}, u32[]{:S(2)}) %collective-permute-start.2) | collective-permute-done | bytes 64 | tf_op jit(solution)/shard_map/ppermute | solution.py:286
  43.6 2.9 %collective-permute-start.5 = (f32[1,8]{1,0:T(1,128)S(1)}, f32[1,8]{1,0:T(1,128)S(1)}, u32[]{:S(2)}, u32[]{:S(2)}) collective-permute-start(f32[1,8]{1,0:T(1,128)S(1)} %add.12), channel_id=1, source_target_pairs={{0,4},{1,5},{2,6},{3,7},{4,0},{5,1},{6,2},{7,3},{8,12},{9,13},{10,... | collective-permute-start | bytes 104 | tf_op jit(solution)/shard_map/ppermute | solution.py:288
  46.6 0.8 %collective-permute-start.4 = (f32[1,8]{1,0:T(1,128)S(1)}, f32[1,8]{1,0:T(1,128)S(1)}, u32[]{:S(2)}, u32[]{:S(2)}) collective-permute-start(f32[1,8]{1,0:T(1,128)S(1)} %add.12), channel_id=1, source_target_pairs={{0,6},{1,7},{2,0},{3,1},{4,2},{5,3},{6,4},{7,5},{8,14},{9,15},{10,... | collective-permute-start | bytes 104 | tf_op jit(solution)/shard_map/ppermute | solution.py:288
  47.3 0.7 %collective-permute-start.3 = (f32[1,8]{1,0:T(1,128)S(1)}, f32[1,8]{1,0:T(1,128)S(1)}, u32[]{:S(2)}, u32[]{:S(2)}) collective-permute-start(f32[1,8]{1,0:T(1,128)S(1)} %add.12), channel_id=1, source_target_pairs={{0,2},{1,3},{2,4},{3,5},{4,6},{5,7},{6,0},{7,1},{8,10},{9,11},{10,... | collective-permute-start | bytes 104 | tf_op jit(solution)/shard_map/ppermute | solution.py:288
  48.0 0.0 collective-permute-done.5
  48.0 0.9 %collective-permute-done.4 = f32[1,8]{1,0:T(1,128)S(1)} collective-permute-done((f32[1,8]{1,0:T(1,128)S(1)}, f32[1,8]{1,0:T(1,128)S(1)}, u32[]{:S(2)}, u32[]{:S(2)}) %collective-permute-start.4) | collective-permute-done | bytes 64 | tf_op jit(solution)/shard_map/ppermute | solution.py:288
  49.0 2.0 %collective-permute-done.3 = f32[1,8]{1,0:T(1,128)S(1)} collective-permute-done((f32[1,8]{1,0:T(1,128)S(1)}, f32[1,8]{1,0:T(1,128)S(1)}, u32[]{:S(2)}, u32[]{:S(2)}) %collective-permute-start.3) | collective-permute-done | bytes 64 | tf_op jit(solution)/shard_map/ppermute | solution.py:288
  50.9 0.5 %add_bitcast_fusion = f32[8]{0:T(128)} fusion(f32[1,8]{1,0:T(1,128)S(1)} %add.12, f32[1,8]{1,0:T(1,128)S(1)} %collective-permute-done.5, f32[1,8]{1,0:T(1,128)S(1)} %collective-permute-done.3, f32[1,8]{1,0:T(1,128)S(1)} %collective-permute-done.4), kind=kLoop, calls=%fused_computation | loop fusion | flops 24 | bytes 160 | tf_op jit(solution)/shard_map/squeeze | solution.py:291
  (1 shorter events, 0.0 us)
Async XLA Ops:
  2.0 14.6 %collective-permute-start.1 = (bf16[9,256,128]{2,1,0:T(8,128)(2,1)S(1)}, bf16[9,256,128]{2,1,0:T(8,128)(2,1)S(1)}, u32[]{:S(2)}, u32[]{:S(2)}) collective-permute-start(bf16[9,256,128]{2,1,0:T(8,128)(2,1)S(1)} %get-tuple-element.11), channel_id=1, source_target_pairs={{0,8},{8,0},{16,24},{24,16},{32,40},{40,32},{48,56},{56,48},{64,72... | collective-permute-start | bytes 1769480 | tf_op jit(solution)/shard_map/ppermute | solution.py:268
  4.6 12.5 %collective-permute-start = (bf16[9,256,128]{2,1,0:T(8,128)(2,1)S(1)}, bf16[9,256,128]{2,1,0:T(8,128)(2,1)S(1)}, u32[]{:S(2)}, u32[]{:S(2)}) collective-permute-start(bf16[9,256,128]{2,1,0:T(8,128)(2,1)S(1)} %get-tuple-element.9), channel_id=1, source_target_pairs={{0,1},{1,0},{2,3},{3,2},{4,5},{5,4},{6,7},{7,6},{8,16},{9,17},{10,... | collective-permute-start | bytes 1769480 | tf_op jit(solution)/shard_map/ppermute | solution.py:269
  39.5 4.1 %collective-permute-start.2 = (f32[1,8]{1,0:T(1,128)S(1)}, f32[1,8]{1,0:T(1,128)S(1)}, u32[]{:S(2)}, u32[]{:S(2)}) collective-permute-start(f32[1,8]{1,0:T(1,128)S(1)} %get-tuple-element.15), channel_id=1, source_target_pairs={{0,1},{1,0},{2,3},{3,2},{4,5},{5,4},{6,7},{7,6},{8,9},{9,8},{10,11... | collective-permute-start | bytes 104 | tf_op jit(solution)/shard_map/ppermute | solution.py:286
  43.6 4.4 %collective-permute-start.5 = (f32[1,8]{1,0:T(1,128)S(1)}, f32[1,8]{1,0:T(1,128)S(1)}, u32[]{:S(2)}, u32[]{:S(2)}) collective-permute-start(f32[1,8]{1,0:T(1,128)S(1)} %add.12), channel_id=1, source_target_pairs={{0,4},{1,5},{2,6},{3,7},{4,0},{5,1},{6,2},{7,3},{8,12},{9,13},{10,... | collective-permute-start | bytes 104 | tf_op jit(solution)/shard_map/ppermute | solution.py:288
  46.6 2.4 %collective-permute-start.4 = (f32[1,8]{1,0:T(1,128)S(1)}, f32[1,8]{1,0:T(1,128)S(1)}, u32[]{:S(2)}, u32[]{:S(2)}) collective-permute-start(f32[1,8]{1,0:T(1,128)S(1)} %add.12), channel_id=1, source_target_pairs={{0,6},{1,7},{2,0},{3,1},{4,2},{5,3},{6,4},{7,5},{8,14},{9,15},{10,... | collective-permute-start | bytes 104 | tf_op jit(solution)/shard_map/ppermute | solution.py:288
  47.3 3.6 %collective-permute-start.3 = (f32[1,8]{1,0:T(1,128)S(1)}, f32[1,8]{1,0:T(1,128)S(1)}, u32[]{:S(2)}, u32[]{:S(2)}) collective-permute-start(f32[1,8]{1,0:T(1,128)S(1)} %add.12), channel_id=1, source_target_pairs={{0,2},{1,3},{2,4},{3,5},{4,6},{5,7},{6,0},{7,1},{8,10},{9,11},{10,... | collective-permute-start | bytes 104 | tf_op jit(solution)/shard_map/ppermute | solution.py:288
